TPU v7x, 256 devices: a whole 4x4x8 slice. The times are simulated.
256 devices in a mesh: blk: 64 (over y, x_lo, z), rep: 4 (over x_hi, core).
Axes of the slice: x: 4 (x_hi: 2, x_lo: 2; x = x_hi * 2 + x_lo), y: 4, z: 8, core: 2. Of those that a mesh axis runs over, the one named last changes fastest.
Arguments:
- image_feats: bfloat16 [131072, 1152], P(('blk', 'rep')), may hold values from -16 to 16, as said below
- text_feats: bfloat16 [131072, 1152], P(('blk', 'rep')), may hold values from -16 to 16, as said below
- head: bfloat16 [1152, 1152], replicated, may hold values from -0.1875 to 0.1875
- image_ids: int32 [131072], P(('blk', 'rep')), may hold values from 0 to 2047
- text_ids: int32 [131072], P(('blk', 'rep')), may hold values from 0 to 2047
- log_scale: float32 [1], replicated, may hold values from 3 to 3.7
- bias: float32 [1], replicated, may hold values from -3 to -1
Outputs:
- grad_image_feats: bfloat16 [131072, 1152], P(('blk', 'rep'))
- grad_text_feats: bfloat16 [131072, 1152], P(('blk', 'rep'))
- grad_head: float32 [1152, 1152], P('blk')
Inputs may be any that keep to these rules, and one draw needn't show every extreme that they name: `image_feats`: row magnitudes differ from row to row. `text_feats`: row magnitudes differ from row to row.
All inputs are finite; a program needn't handle non-finite values.
Results may differ from a plain program's by a relative error of at most 0.0072.
Values may be sent and summed in bfloat16 or wider, within the bound.
No kernel may reach another device: no remote copies, remote signals or barrier semaphores. Data moves between devices by JAX's collectives and lax.ppermute only.
A program may use at most 128 MiB of HBM per device.

v0:
```python
import jax
import jax.numpy as jnp
from jax import lax
from jax.sharding import PartitionSpec as P

HOPS = 4


def shifted(value, axis, steps):
    count = lax.axis_size(axis)
    pairs = [(source, (source + steps) % count) for source in range(count)]
    return lax.ppermute(value, axis, pairs)


def unit_rows(values):
    inverse = lax.rsqrt(jnp.sum(values * values, axis=-1, keepdims=True) + 1e-06)
    return (values * inverse, inverse)


def per_device(image_feats, text_feats, head, image_ids, text_ids, log_scale, bias):
    u_local = jnp.dot(image_feats, head, preferred_element_type=jnp.float32)
    x_full, inv_u = unit_rows(u_local)
    x_half = x_full.astype(jnp.bfloat16)
    y_full, inv_t = unit_rows(text_feats.astype(jnp.float32))
    y_half = y_full.astype(jnp.bfloat16)
    scale = jnp.exp(log_scale[0])
    offset = bias[0]

    def coefficients(images, image_labels, texts, text_labels):
        logits = (
            scale * jnp.einsum("id,jd->ij", images, texts, preferred_element_type=jnp.float32)
            + offset
        )
        positive = (image_labels[:, None] == text_labels[None, :]).astype(jnp.float32)
        return (scale * (jax.nn.sigmoid(logits) - positive)).astype(jnp.bfloat16)

    def tile(block, block_ids):
        coef = coefficients(x_half, image_ids, block, block_ids)
        image_part = jnp.dot(coef, block, preferred_element_type=jnp.float32)
        text_part = jnp.einsum("ij,id->jd", coef, x_half, preferred_element_type=jnp.float32)
        return (image_part, text_part)

    grad_x, text_sum = tile(y_half, text_ids)
    block, block_ids = (y_half, text_ids)
    for hop in range(1, HOPS + 1):
        block = shifted(block, "blk", 1)
        block_ids = shifted(block_ids, "blk", 1)
        image_part, text_part = tile(block, block_ids)
        grad_x = grad_x + image_part
        text_sum = shifted(text_sum, "blk", 1) + text_part
    grad_y = shifted(text_sum, "blk", -HOPS)
    grad_u = (inv_u * (grad_x - x_full * jnp.sum(x_full * grad_x, axis=1, keepdims=True))).astype(
        jnp.bfloat16
    )
    grad_image = jnp.einsum("id,ed->ie", grad_u, head, preferred_element_type=jnp.float32).astype(
        jnp.bfloat16
    )
    cycle_rows = lax.psum_scatter(
        jnp.einsum("ie,id->ed", image_feats, grad_u, preferred_element_type=jnp.float32),
        "blk",
        scatter_dimension=0,
        tiled=True,
    )
    devices_all = lax.axis_size("blk") * lax.axis_size("rep")
    grad_head = lax.psum(cycle_rows, "rep") / devices_all
    grad_text = (
        inv_t * (grad_y - y_full * jnp.sum(y_full * grad_y, axis=1, keepdims=True))
    ).astype(jnp.bfloat16)
    return (grad_image, grad_text, grad_head)


def solution(mesh):
    placed = (
        P(("blk", "rep"), None),
        P(("blk", "rep"), None),
        P(),
        P(("blk", "rep")),
        P(("blk", "rep")),
        P(),
        P(),
    )
    return jax.shard_map(
        per_device,
        mesh=mesh,
        in_specs=placed,
        out_specs=(P(("blk", "rep"), None), P(("blk", "rep"), None), P("blk", None)),
        check_vma=False,
    )
```

profile of v0, /device:TPU:1, one launch (start us, length us, event | category | flops | bytes accessed | tf_op | source)
XLA Modules:
  0.0 1003.0 jit_solution(10093257569630580109)
XLA Ops:
  7.2 1.7 fusion.7
  9.0 0.3 fusion.2
  9.3 2.5 collective-permute-start
  11.8 2.0 multiply_reduce_fusion.1
  15.2 0.2 multiply_convert_fusion.1
  15.4 0.4 copy-done.9
  15.8 1.1 fusion.43
  16.9 0.9 fusion.49
  17.8 1.7 collective-permute-start.8
  19.5 25.3 %collective-permute-done = bf16[512,1152]{1,0:T(8,128)(2,1)S(1)} collective-permute-done((bf16[512,1152]{1,0:T(8,128)(2,1)S(1)}, bf16[512,1152]{1,0:T(8,128)(2,1)S(1)}, u32[]{:S(2)}, u32[]{:S(2)}) %collective-permute-start) | collective-permute-done | bytes 1179680 | tf_op jit(solution)/shard_map/ppermute | solution.py:12
  44.8 75.9 %collective-permute-done.1 = s32[512]{0:T(512)S(1)} collective-permute-done((s32[512]{0:T(512)S(1)}, s32[512]{0:T(512)S(1)}, u32[]{:S(2)}, u32[]{:S(2)}) %collective-permute-start.1) | collective-permute-done | bytes 2080 | tf_op jit(solution)/shard_map/ppermute | solution.py:12
  120.7 6.7 collective-permute-done.3
  127.4 1.1 fusion.44
  128.6 0.9 convolution_add_fusion
  129.5 0.3 collective-permute-start.9
  129.7 0.8 fusion.48
  130.6 3.4 collective-permute-done.5
  134.0 0.9 convolution_add_fusion.4
  134.9 1.1 fusion.45
  136.0 21.9 %collective-permute-done.4 = bf16[512,1152]{1,0:T(8,128)(2,1)S(1)} collective-permute-done((bf16[512,1152]{1,0:T(8,128)(2,1)S(1)}, bf16[512,1152]{1,0:T(8,128)(2,1)S(1)}, u32[]{:S(2)}, u32[]{:S(2)}) %collective-permute-start.4) | collective-permute-done | bytes 1179680 | tf_op jit(solution)/shard_map/ppermute | solution.py:12
  157.9 0.9 fusion.50
  158.8 0.9 convolution_add_fusion.3
  159.6 1.1 fusion.46
  160.7 0.9 convolution_add_fusion.2
  161.6 46.8 %collective-permute-done.9 = f32[512,1152]{1,0:T(8,128)S(1)} collective-permute-done((f32[512,1152]{1,0:T(8,128)S(1)}, f32[512,1152]{1,0:T(8,128)S(1)}, u32[]{:S(2)}, u32[]{:S(2)}) %collective-permute-start.9) | collective-permute-done | bytes 2359328 | tf_op jit(solution)/shard_map/ppermute | solution.py:12
  208.5 1.7 add.99
  210.2 23.6 %collective-permute-done.6 = bf16[512,1152]{1,0:T(8,128)(2,1)S(1)} collective-permute-done((bf16[512,1152]{1,0:T(8,128)(2,1)S(1)}, bf16[512,1152]{1,0:T(8,128)(2,1)S(1)}, u32[]{:S(2)}, u32[]{:S(2)}) %collective-permute-start.6) | collective-permute-done | bytes 1179680 | tf_op jit(solution)/shard_map/ppermute | solution.py:12
  233.8 1.1 fusion.47
  234.9 1.1 multiply_reduce_fusion
  236.0 0.4 multiply_convert_fusion
  236.4 1.0 copy-done.5
  237.4 4.1 convolution_bitcast_fusion
  241.6 2.1 fusion.51
  243.8 47.0 %collective-permute-done.10 = f32[512,1152]{1,0:T(8,128)} collective-permute-done((f32[512,1152]{1,0:T(8,128)}, f32[512,1152]{1,0:T(8,128)}, u32[]{:S(2)}, u32[]{:S(2)}) %collective-permute-start.10) | collective-permute-done | bytes 2359328 | tf_op jit(solution)/shard_map/ppermute | solution.py:12
  290.8 2.0 add.100
  292.8 0.3 collective-permute-start.11
  293.1 0.9 fusion.52
  294.0 65.8 %collective-permute-done.11 = f32[512,1152]{1,0:T(8,128)S(1)} collective-permute-done((f32[512,1152]{1,0:T(8,128)S(1)}, f32[512,1152]{1,0:T(8,128)S(1)}, u32[]{:S(2)}, u32[]{:S(2)}) %collective-permute-start.11) | collective-permute-done | bytes 2359328 | tf_op jit(solution)/shard_map/ppermute | solution.py:12
  359.8 1.7 add.101
  361.5 0.6 dynamic-slice
  362.8 539.7 %all-reduce.6.cloned.1.call-done = f32[1152,1152]{0,1:T(8,128)} async-done(((f32[1152,1152]{0,1:T(8,128)}), f32[1152,1152]{0,1:T(8,128)}) %all-reduce.6.cloned.1.call-update) | async-done | bytes 5308432
  902.5 2.3 constant_dynamic-slice_fusion
  904.8 4.1 convolution_convert_fusion
  909.0 79.4 %all-reduce.4.cloned.1.call-done = f32[18,1152]{0,1:T(8,128)} async-done(((f32[18,1152]{0,1:T(8,128)}), f32[18,1152]{0,1:T(8,128)}) %all-reduce.4.cloned.1.call-update) | async-done | bytes 82960 | tf_op jit(solution)/shard_map/psum | solution.py:65
  988.4 1.1 broadcast_multiply_fusion
  989.6 0.9 copy.11
  990.4 2.5 fusion.3
  993.0 3.2 fusion.6
  (41 shorter events, 0.3 us)
Async XLA Ops:
  7.2 4.7 copy-start
  7.2 895.3 %all-reduce.6.cloned.1.call-start = ((), (), s32[]{:S(2)}) async-start(), calls=%async_computation.1 | async-start | bytes 10616832
  7.2 1.8 copy-start.3
  9.0 2.8 copy-start.8
  9.3 35.6 %collective-permute-start = (bf16[512,1152]{1,0:T(8,128)(2,1)S(1)}, bf16[512,1152]{1,0:T(8,128)(2,1)S(1)}, u32[]{:S(2)}, u32[]{:S(2)}) collective-permute-start(bf16[512,1152]{1,0:T(8,128)(2,1)S(1)} %fusion.2), channel_id=1, source_target_pairs={{0,4},{4,8},{8,12},{12,16},{16,20},{20,24},{24,28},{28,32},{32,36}... | collective-permute-start | bytes 3538952 | tf_op jit(solution)/shard_map/ppermute | solution.py:12
  15.1 0.7 copy-start.9
  15.2 0.7 copy-start.10
  15.4 218.4 %copy-start.1 = (bf16[512,1152]{1,0:T(8,128)(2,1)}, bf16[512,1152]{1,0:T(8,128)(2,1)S(1)}, u32[]{:S(2)}) copy-start(bf16[512,1152]{1,0:T(8,128)(2,1)S(1)} %multiply_convert_fusion.1) | copy-start | bytes 3538948
  17.8 110.7 %collective-permute-start.8 = (f32[512,1152]{1,0:T(8,128)S(1)}, f32[512,1152]{1,0:T(8,128)S(1)}, u32[]{:S(2)}, u32[]{:S(2)}) collective-permute-start(f32[512,1152]{1,0:T(8,128)S(1)} %fusion.49), channel_id=1, source_target_pairs={{0,4},{4,8},{8,12},{12,16},{16,20},{20,24},{24,28},{28,32},{32,36}... | collective-permute-start | bytes 7077896 | tf_op jit(solution)/shard_map/ppermute | solution.py:12
  44.8 83.6 %collective-permute-start.2 = (bf16[512,1152]{1,0:T(8,128)(2,1)S(1)}, bf16[512,1152]{1,0:T(8,128)(2,1)S(1)}, u32[]{:S(2)}, u32[]{:S(2)}) collective-permute-start(bf16[512,1152]{1,0:T(8,128)(2,1)S(1)} %collective-permute-done), channel_id=1, source_target_pairs={{0,4},{4,8},{8,12},{12,16},{16,20},{20,24},{24,28},{28,32},{32,36}... | collective-permute-start | bytes 3538952 | tf_op jit(solution)/shard_map/ppermute | solution.py:12
  44.8 75.9 %collective-permute-start.1 = (s32[512]{0:T(512)S(1)}, s32[512]{0:T(512)S(1)}, u32[]{:S(2)}, u32[]{:S(2)}) collective-permute-start(s32[512]{0:T(512)S(1)} %copy-done.9), channel_id=1, source_target_pairs={{0,4},{4,8},{8,12},{12,16},{16,20},{20,24},{24,28},{28,32},{32,36}... | collective-permute-start | bytes 6152 | tf_op jit(solution)/shard_map/ppermute | solution.py:12
  120.7 6.7 collective-permute-start.3
  127.4 6.7 collective-permute-start.5
  128.5 29.4 %collective-permute-start.4 = (bf16[512,1152]{1,0:T(8,128)(2,1)S(1)}, bf16[512,1152]{1,0:T(8,128)(2,1)S(1)}, u32[]{:S(2)}, u32[]{:S(2)}) collective-permute-start(bf16[512,1152]{1,0:T(8,128)(2,1)S(1)} %collective-permute-done.2), channel_id=1, source_target_pairs={{0,4},{4,8},{8,12},{12,16},{16,20},{20,24},{24,28},{28,32},{32,36}... | collective-permute-start | bytes 3538952 | tf_op jit(solution)/shard_map/ppermute | solution.py:12
  129.5 79.0 %collective-permute-start.9 = (f32[512,1152]{1,0:T(8,128)S(1)}, f32[512,1152]{1,0:T(8,128)S(1)}, u32[]{:S(2)}, u32[]{:S(2)}) collective-permute-start(f32[512,1152]{1,0:T(8,128)S(1)} %convolution_add_fusion), channel_id=1, source_target_pairs={{0,4},{4,8},{8,12},{12,16},{16,20},{20,24},{24,28},{28,32},{32,36}... | collective-permute-start | bytes 7077896 | tf_op jit(solution)/shard_map/ppermute | solution.py:12
  134.0 76.1 %collective-permute-start.7 = (s32[512]{0:T(512)S(1)}, s32[512]{0:T(512)S(1)}, u32[]{:S(2)}, u32[]{:S(2)}) collective-permute-start(s32[512]{0:T(512)S(1)} %collective-permute-done.5), channel_id=1, source_target_pairs={{0,4},{4,8},{8,12},{12,16},{16,20},{20,24},{24,28},{28,32},{32,36}... | collective-permute-start | bytes 6152 | tf_op jit(solution)/shard_map/ppermute | solution.py:12
  157.9 75.9 %collective-permute-start.6 = (bf16[512,1152]{1,0:T(8,128)(2,1)S(1)}, bf16[512,1152]{1,0:T(8,128)(2,1)S(1)}, u32[]{:S(2)}, u32[]{:S(2)}) collective-permute-start(bf16[512,1152]{1,0:T(8,128)(2,1)S(1)} %collective-permute-done.4), channel_id=1, source_target_pairs={{0,4},{4,8},{8,12},{12,16},{16,20},{20,24},{24,28},{28,32},{32,36}... | collective-permute-start | bytes 3538952 | tf_op jit(solution)/shard_map/ppermute | solution.py:12
  210.2 80.6 %collective-permute-start.10 = (f32[512,1152]{1,0:T(8,128)}, f32[512,1152]{1,0:T(8,128)}, u32[]{:S(2)}, u32[]{:S(2)}) collective-permute-start(f32[512,1152]{1,0:T(8,128)} %add.99), channel_id=1, source_target_pairs={{0,4},{4,8},{8,12},{12,16},{16,20},{20,24},{24,28},{28,32},{32,36}... | collective-permute-start | bytes 7077896 | tf_op jit(solution)/shard_map/ppermute | solution.py:12
  234.9 1.1 copy-start.6
  236.4 1.0 copy-start.5
  241.6 746.9 %all-reduce.4.cloned.1.call-start = ((), (), s32[]{:S(2)}) async-start(), calls=%async_computation | async-start | bytes 1179648 | tf_op jit(solution)/shard_map/psum | solution.py:65
  243.8 49.3 %copy-start.2 = (bf16[512,1152]{1,0:T(8,128)(2,1)S(1)}, bf16[512,1152]{1,0:T(8,128)(2,1)}, u32[]{:S(2)}) copy-start(bf16[512,1152]{1,0:T(8,128)(2,1)} %copy-done.1) | copy-start | bytes 3538948
  243.8 49.3 %copy-start.7 = (bf16[512,512]{1,0:T(8,128)(2,1)S(1)}, bf16[512,512]{1,0:T(8,128)(2,1)}, u32[]{:S(2)}) copy-start(bf16[512,512]{1,0:T(8,128)(2,1)} %copy-done.6) | copy-start | bytes 1572868
  292.8 67.1 %collective-permute-start.11 = (f32[512,1152]{1,0:T(8,128)S(1)}, f32[512,1152]{1,0:T(8,128)S(1)}, u32[]{:S(2)}, u32[]{:S(2)}) collective-permute-start(f32[512,1152]{1,0:T(8,128)S(1)} %add.100), channel_id=1, source_target_pairs={{0,4},{4,8},{8,12},{12,16},{16,20},{20,24},{24,28},{28,32},{32,36}... | collective-permute-start | bytes 7077896 | tf_op jit(solution)/shard_map/ppermute | solution.py:12
  294.0 67.6 %copy-start.11 = (u32[256]{0:T(256)S(1)}, u32[256]{0:T(256)}, u32[]{:S(2)}) copy-start(u32[256]{0:T(256)} %constant.11) | copy-start | bytes 3076
  361.5 628.9 %collective-permute-start.12 = (f32[512,1152]{1,0:T(8,128)}, f32[512,1152]{1,0:T(8,128)}, u32[]{:S(2)}, u32[]{:S(2)}) collective-permute-start(f32[512,1152]{1,0:T(8,128)} %add.101), channel_id=1, source_target_pairs={{0,240},{4,244},{8,248},{12,252},{16,0},{20,4},{24,8},{28,12},{32,... | collective-permute-start | bytes 7077896 | tf_op jit(solution)/shard_map/ppermute | solution.py:12
  990.4 2.5 copy-start.4
Sparse Core Ops, SparseCore 0:
  241.7 660.7 all-reduce.5
  905.1 83.2 all-reduce.3
where the time goes:
time: 1000 us
  waiting for transfers between devices  936 us (94%)
  matrix products  25.8 us (3%)
  between operations  16.3 us (2%)
  other arithmetic  14.8 us (1%)
    unnamed x3, waiting for transfers between devices  540 us
    ppermute x13, waiting for transfers between devices, shifted(): return lax.ppermute(value, axis, pairs)  316 us
    psum x1, waiting for transfers between devices, per_device(): grad_head = lax.psum(cycle_rows, 'rep') / devices_all  79.4 us
  transfers between devices with their start and end apart: 15, of which 11 were waited for; matrix products, arithmetic and copies ran while one was open for 4% of the time, Pallas kernels for 0%

commit v1 on v0

--- a/solution.py
+++ b/solution.py
@@ -18,6 +18,10 @@
 
 
 def per_device(image_feats, text_feats, head, image_ids, text_ids, log_scale, bias):
+
+    def apply_entries(tile_in, shard_axis):
+        return jnp.sum(lax.all_gather(tile_in, shard_axis), axis=0)
+
     u_local = jnp.dot(image_feats, head, preferred_element_type=jnp.float32)
     x_full, inv_u = unit_rows(u_local)
     x_half = x_full.astype(jnp.bfloat16)
@@ -62,7 +66,7 @@
         tiled=True,
     )
     devices_all = lax.axis_size("blk") * lax.axis_size("rep")
-    grad_head = lax.psum(cycle_rows, "rep") / devices_all
+    grad_head = apply_entries(cycle_rows, "rep") / devices_all
     grad_text = (
         inv_t * (grad_y - y_full * jnp.sum(y_full * grad_y, axis=1, keepdims=True))
     ).astype(jnp.bfloat16)

time: 1000 us -> 968 us (0.968)
  waiting for transfers between devices: 936 us -> 852 us
  blocking collectives: 0 us -> 48.2 us
    psum x1 -> x0, waiting for transfers between devices: 79.4 us -> none  [per_device(): grad_head = lax.psum(cycle_rows, 'rep') / devices_all]
    all_gather x0 -> x1, blocking collectives: none -> 48.2 us  [apply_entries(): return jnp.sum(lax.all_gather(tile_in, shard_axis), axis=0)]
    unnamed x3 -> x2, waiting for transfers between devices: 540 us -> 535 us
  transfers between devices with their start and end apart: 15 -> 14, of which waited for: 11 -> 10; matrix products, arithmetic and copies ran while one was open for 4% -> 4% of each run, Pallas kernels for 0% -> 0%
where the time goes in v1:
time: 968 us
  waiting for transfers between devices  852 us (88%)
  blocking collectives  48.2 us (5%)
  matrix products  25.8 us (3%)
  between operations  16.3 us (2%)
  other arithmetic  14.6 us (2%)
    unnamed x2, waiting for transfers between devices  535 us
    ppermute x13, waiting for transfers between devices, shifted(): return lax.ppermute(value, axis, pairs)  317 us
    all_gather x1, blocking collectives, apply_entries(): return jnp.sum(lax.all_gather(tile_in, shard_axis), axis=0)  48.2 us
  transfers between devices with their start and end apart: 14, of which 10 were waited for; matrix products, arithmetic and copies ran while one was open for 4% of the time, Pallas kernels for 0%

profile of v1, /device:TPU:1, one launch (start us, length us, event | category | flops | bytes accessed | tf_op | source)
XLA Modules:
  0.0 968.0 jit_solution(9709102906618435654)
XLA Ops:
  7.2 1.7 fusion.7
  9.0 0.3 fusion.2
  9.3 2.5 collective-permute-start
  11.8 2.0 multiply_reduce_fusion.1
  15.4 0.4 copy-done.9
  15.8 1.1 fusion.43
  16.9 0.9 fusion.49
  17.8 1.7 collective-permute-start.8
  19.5 25.3 %collective-permute-done = bf16[512,1152]{1,0:T(8,128)(2,1)S(1)} collective-permute-done((bf16[512,1152]{1,0:T(8,128)(2,1)S(1)}, bf16[512,1152]{1,0:T(8,128)(2,1)S(1)}, u32[]{:S(2)}, u32[]{:S(2)}) %collective-permute-start) | collective-permute-done | bytes 1179680 | tf_op jit(solution)/shard_map/ppermute | solution.py:12
  44.8 75.9 %collective-permute-done.1 = s32[512]{0:T(512)S(1)} collective-permute-done((s32[512]{0:T(512)S(1)}, s32[512]{0:T(512)S(1)}, u32[]{:S(2)}, u32[]{:S(2)}) %collective-permute-start.1) | collective-permute-done | bytes 2080 | tf_op jit(solution)/shard_map/ppermute | solution.py:12
  120.7 6.7 collective-permute-done.3
  127.4 1.1 fusion.44
  128.6 0.9 convolution_add_fusion
  129.5 0.3 collective-permute-start.9
  129.7 0.8 fusion.48
  130.6 3.4 collective-permute-done.5
  134.0 0.9 convolution_add_fusion.4
  134.9 1.1 fusion.45
  136.0 21.9 %collective-permute-done.4 = bf16[512,1152]{1,0:T(8,128)(2,1)S(1)} collective-permute-done((bf16[512,1152]{1,0:T(8,128)(2,1)S(1)}, bf16[512,1152]{1,0:T(8,128)(2,1)S(1)}, u32[]{:S(2)}, u32[]{:S(2)}) %collective-permute-start.4) | collective-permute-done | bytes 1179680 | tf_op jit(solution)/shard_map/ppermute | solution.py:12
  157.9 0.9 fusion.50
  158.8 0.8 convolution_add_fusion.3
  159.6 1.1 fusion.46
  160.7 0.9 convolution_add_fusion.2
  161.6 46.8 %collective-permute-done.9 = f32[512,1152]{1,0:T(8,128)S(1)} collective-permute-done((f32[512,1152]{1,0:T(8,128)S(1)}, f32[512,1152]{1,0:T(8,128)S(1)}, u32[]{:S(2)}, u32[]{:S(2)}) %collective-permute-start.9) | collective-permute-done | bytes 2359328 | tf_op jit(solution)/shard_map/ppermute | solution.py:12
  208.5 1.7 add.97
  210.2 23.6 %collective-permute-done.6 = bf16[512,1152]{1,0:T(8,128)(2,1)S(1)} collective-permute-done((bf16[512,1152]{1,0:T(8,128)(2,1)S(1)}, bf16[512,1152]{1,0:T(8,128)(2,1)S(1)}, u32[]{:S(2)}, u32[]{:S(2)}) %collective-permute-start.6) | collective-permute-done | bytes 1179680 | tf_op jit(solution)/shard_map/ppermute | solution.py:12
  233.8 1.1 fusion.47
  234.9 1.1 multiply_reduce_fusion
  236.0 0.4 multiply_convert_fusion
  236.4 1.0 copy-done.5
  237.4 4.1 convolution_bitcast_fusion
  241.6 2.1 fusion.51
  243.7 47.0 %collective-permute-done.10 = f32[512,1152]{1,0:T(8,128)} collective-permute-done((f32[512,1152]{1,0:T(8,128)}, f32[512,1152]{1,0:T(8,128)}, u32[]{:S(2)}, u32[]{:S(2)}) %collective-permute-start.10) | collective-permute-done | bytes 2359328 | tf_op jit(solution)/shard_map/ppermute | solution.py:12
  290.8 2.0 add.98
  292.8 0.3 collective-permute-start.11
  293.1 0.9 fusion.52
  294.0 66.1 %collective-permute-done.11 = f32[512,1152]{1,0:T(8,128)S(1)} collective-permute-done((f32[512,1152]{1,0:T(8,128)S(1)}, f32[512,1152]{1,0:T(8,128)S(1)}, u32[]{:S(2)}, u32[]{:S(2)}) %collective-permute-start.11) | collective-permute-done | bytes 2359328 | tf_op jit(solution)/shard_map/ppermute | solution.py:12
  360.1 1.7 add.99
  361.8 0.6 dynamic-slice
  363.0 4.2 convolution_convert_fusion
  367.2 535.3 %all-reduce.3.cloned.1.call-done = f32[1152,1152]{0,1:T(8,128)} async-done(((f32[1152,1152]{0,1:T(8,128)}), f32[1152,1152]{0,1:T(8,128)}) %all-reduce.3.cloned.1.call-update) | async-done | bytes 5308432
  902.5 1.5 dynamic-slice_bitcast_fusion
  904.2 48.2 %all-gather.1 = f32[4,18,1152]{2,1,0:T(8,128)S(1)} all-gather(f32[1,18,1152]{2,1,0:T(8,128)S(1)} %copy.10), channel_id=2, replica_groups=mesh['blk'=64,'rep'=4] {'rep'}, dimensions={0}, use_global_device_ids=true | all-gather | bytes 414720 | tf_op jit(solution)/shard_map/all_gather | solution.py:23
  952.4 0.2 copy.15
  952.6 0.9 broadcast_multiply_fusion
  953.5 1.9 copy.12
  955.4 2.5 fusion.3
  958.0 3.2 fusion.6
  (42 shorter events, 0.7 us)
Async XLA Ops:
  7.2 4.7 copy-start
  7.2 895.3 %all-reduce.3.cloned.1.call-start = ((), (), s32[]{:S(2)}) async-start(), calls=%async_computation | async-start | bytes 10616832
  7.2 1.8 copy-start.3
  9.0 2.8 copy-start.8
  9.3 35.6 %collective-permute-start = (bf16[512,1152]{1,0:T(8,128)(2,1)S(1)}, bf16[512,1152]{1,0:T(8,128)(2,1)S(1)}, u32[]{:S(2)}, u32[]{:S(2)}) collective-permute-start(bf16[512,1152]{1,0:T(8,128)(2,1)S(1)} %fusion.2), channel_id=1, source_target_pairs={{0,4},{4,8},{8,12},{12,16},{16,20},{20,24},{24,28},{28,32},{32,36}... | collective-permute-start | bytes 3538952 | tf_op jit(solution)/shard_map/ppermute | solution.py:12
  15.1 0.7 copy-start.9
  15.2 0.7 copy-start.10
  15.4 218.4 %copy-start.1 = (bf16[512,1152]{1,0:T(8,128)(2,1)}, bf16[512,1152]{1,0:T(8,128)(2,1)S(1)}, u32[]{:S(2)}) copy-start(bf16[512,1152]{1,0:T(8,128)(2,1)S(1)} %multiply_convert_fusion.1) | copy-start | bytes 3538948
  17.8 110.7 %collective-permute-start.8 = (f32[512,1152]{1,0:T(8,128)S(1)}, f32[512,1152]{1,0:T(8,128)S(1)}, u32[]{:S(2)}, u32[]{:S(2)}) collective-permute-start(f32[512,1152]{1,0:T(8,128)S(1)} %fusion.49), channel_id=1, source_target_pairs={{0,4},{4,8},{8,12},{12,16},{16,20},{20,24},{24,28},{28,32},{32,36}... | collective-permute-start | bytes 7077896 | tf_op jit(solution)/shard_map/ppermute | solution.py:12
  44.8 83.6 %collective-permute-start.2 = (bf16[512,1152]{1,0:T(8,128)(2,1)S(1)}, bf16[512,1152]{1,0:T(8,128)(2,1)S(1)}, u32[]{:S(2)}, u32[]{:S(2)}) collective-permute-start(bf16[512,1152]{1,0:T(8,128)(2,1)S(1)} %collective-permute-done), channel_id=1, source_target_pairs={{0,4},{4,8},{8,12},{12,16},{16,20},{20,24},{24,28},{28,32},{32,36}... | collective-permute-start | bytes 3538952 | tf_op jit(solution)/shard_map/ppermute | solution.py:12
  44.8 75.9 %collective-permute-start.1 = (s32[512]{0:T(512)S(1)}, s32[512]{0:T(512)S(1)}, u32[]{:S(2)}, u32[]{:S(2)}) collective-permute-start(s32[512]{0:T(512)S(1)} %copy-done.9), channel_id=1, source_target_pairs={{0,4},{4,8},{8,12},{12,16},{16,20},{20,24},{24,28},{28,32},{32,36}... | collective-permute-start | bytes 6152 | tf_op jit(solution)/shard_map/ppermute | solution.py:12
  120.7 6.7 collective-permute-start.3
  127.4 6.7 collective-permute-start.5
  128.5 29.4 %collective-permute-start.4 = (bf16[512,1152]{1,0:T(8,128)(2,1)S(1)}, bf16[512,1152]{1,0:T(8,128)(2,1)S(1)}, u32[]{:S(2)}, u32[]{:S(2)}) collective-permute-start(bf16[512,1152]{1,0:T(8,128)(2,1)S(1)} %collective-permute-done.2), channel_id=1, source_target_pairs={{0,4},{4,8},{8,12},{12,16},{16,20},{20,24},{24,28},{28,32},{32,36}... | collective-permute-start | bytes 3538952 | tf_op jit(solution)/shard_map/ppermute | solution.py:12
  129.5 79.0 %collective-permute-start.9 = (f32[512,1152]{1,0:T(8,128)S(1)}, f32[512,1152]{1,0:T(8,128)S(1)}, u32[]{:S(2)}, u32[]{:S(2)}) collective-permute-start(f32[512,1152]{1,0:T(8,128)S(1)} %convolution_add_fusion), channel_id=1, source_target_pairs={{0,4},{4,8},{8,12},{12,16},{16,20},{20,24},{24,28},{28,32},{32,36}... | collective-permute-start | bytes 7077896 | tf_op jit(solution)/shard_map/ppermute | solution.py:12
  134.0 76.1 %collective-permute-start.7 = (s32[512]{0:T(512)S(1)}, s32[512]{0:T(512)S(1)}, u32[]{:S(2)}, u32[]{:S(2)}) collective-permute-start(s32[512]{0:T(512)S(1)} %collective-permute-done.5), channel_id=1, source_target_pairs={{0,4},{4,8},{8,12},{12,16},{16,20},{20,24},{24,28},{28,32},{32,36}... | collective-permute-start | bytes 6152 | tf_op jit(solution)/shard_map/ppermute | solution.py:12
  157.9 75.9 %collective-permute-start.6 = (bf16[512,1152]{1,0:T(8,128)(2,1)S(1)}, bf16[512,1152]{1,0:T(8,128)(2,1)S(1)}, u32[]{:S(2)}, u32[]{:S(2)}) collective-permute-start(bf16[512,1152]{1,0:T(8,128)(2,1)S(1)} %collective-permute-done.4), channel_id=1, source_target_pairs={{0,4},{4,8},{8,12},{12,16},{16,20},{20,24},{24,28},{28,32},{32,36}... | collective-permute-start | bytes 3538952 | tf_op jit(solution)/shard_map/ppermute | solution.py:12
  210.1 80.6 %collective-permute-start.10 = (f32[512,1152]{1,0:T(8,128)}, f32[512,1152]{1,0:T(8,128)}, u32[]{:S(2)}, u32[]{:S(2)}) collective-permute-start(f32[512,1152]{1,0:T(8,128)} %add.97), channel_id=1, source_target_pairs={{0,4},{4,8},{8,12},{12,16},{16,20},{20,24},{24,28},{28,32},{32,36}... | collective-permute-start | bytes 7077896 | tf_op jit(solution)/shard_map/ppermute | solution.py:12
  234.9 1.1 copy-start.6
  236.4 1.0 copy-start.5
  243.7 49.4 %copy-start.2 = (bf16[512,1152]{1,0:T(8,128)(2,1)S(1)}, bf16[512,1152]{1,0:T(8,128)(2,1)}, u32[]{:S(2)}) copy-start(bf16[512,1152]{1,0:T(8,128)(2,1)} %copy-done.1) | copy-start | bytes 3538948
  243.7 49.4 %copy-start.7 = (bf16[512,512]{1,0:T(8,128)(2,1)S(1)}, bf16[512,512]{1,0:T(8,128)(2,1)}, u32[]{:S(2)}) copy-start(bf16[512,512]{1,0:T(8,128)(2,1)} %copy-done.6) | copy-start | bytes 1572868
  292.8 67.3 %collective-permute-start.11 = (f32[512,1152]{1,0:T(8,128)S(1)}, f32[512,1152]{1,0:T(8,128)S(1)}, u32[]{:S(2)}, u32[]{:S(2)}) collective-permute-start(f32[512,1152]{1,0:T(8,128)S(1)} %add.98), channel_id=1, source_target_pairs={{0,4},{4,8},{8,12},{12,16},{16,20},{20,24},{24,28},{28,32},{32,36}... | collective-permute-start | bytes 7077896 | tf_op jit(solution)/shard_map/ppermute | solution.py:12
  294.0 67.8 %copy-start.11 = (u32[256]{0:T(256)S(1)}, u32[256]{0:T(256)}, u32[]{:S(2)}) copy-start(u32[256]{0:T(256)} %constant.11) | copy-start | bytes 3076
  361.8 593.7 %collective-permute-start.12 = (f32[512,1152]{1,0:T(8,128)}, f32[512,1152]{1,0:T(8,128)}, u32[]{:S(2)}, u32[]{:S(2)}) collective-permute-start(f32[512,1152]{1,0:T(8,128)} %add.99), channel_id=1, source_target_pairs={{0,240},{4,244},{8,248},{12,252},{16,0},{20,4},{24,8},{28,12},{32,... | collective-permute-start | bytes 7077896 | tf_op jit(solution)/shard_map/ppermute | solution.py:12
  955.4 2.5 copy-start.4
Sparse Core Ops, SparseCore 0:
  241.7 660.7 all-reduce.2
